TPU v7x, 512 devices: a whole 4x4x16 slice. The times are simulated.
512 devices in a mesh: seq: 32 (over x, z_lo), head: 8 (over y, core), enc: 2 (over z_hi).
Axes of the slice: x: 4, y: 4, z: 16 (z_hi: 2, z_lo: 8; z = z_hi * 8 + z_lo), core: 2. Of those that a mesh axis runs over, the one named last changes fastest.
Arguments:
- queries: bfloat16 [10240, 4096], P('seq', ('head', 'enc')), may hold values from -2000 to 2000
- keys: bfloat16 [10240, 4096], P('seq', ('head', 'enc')), may hold values from -2000 to 2000
- values: bfloat16 [10240, 4096], P('seq', ('head', 'enc')), may hold values from -6 to 6
- out_weight: bfloat16 [4096, 5120], P(('head', 'enc'), 'seq'), may hold values from -0.1875 to 0.1875
- q_gain: float32 [4096], P(('head', 'enc')), may hold values from 0.75 to 3
- k_gain: float32 [4096], P(('head', 'enc')), may hold values from 0.75 to 3
- gate: float32 [5120], P(('head', 'enc')), may hold values from 1 to 8
- valid_count: int32 [1], replicated, may hold values from 5120 to 10240
Outputs:
- update: bfloat16 [10240, 5120], P('seq', ('head', 'enc'))
Inputs may be any that keep to these rules, and one draw needn't show every extreme that they name: Key positions from valid_count[0] on are padding and take no weight.
All inputs are finite; a program needn't handle non-finite values.
Results may differ from a plain program's by a relative error of at most 0.015.
The roundings to bfloat16 on the way count: a program that leaves them out, or rounds other values in their place, can miss the bound.
Values may be sent and summed in bfloat16 or wider, within the bound.
No kernel may reach another device: no remote copies, remote signals or barrier semaphores. Data moves between devices by JAX's collectives and lax.ppermute only.
A program may use at most 64 MiB of HBM per device.

v0:
```python
import jax
import jax.numpy as jnp
from jax import lax
from jax.sharding import PartitionSpec as P

HEAD_DIM = 128
epsilon = 1e-06
lowest_score = -1e30


def normalize(matrix, squares, gain_row, feature_count):
    inverse_rms = lax.rsqrt(squares / feature_count + epsilon)
    return (matrix.astype(jnp.float32) * inverse_rms[:, None] * gain_row[None, :]).astype(
        jnp.bfloat16
    )


def absorb(carried, query_heads, key_block, value_block, offset, key_limit):
    running_sum, running_max, running_mass = carried
    scale_factor = query_heads.shape[2] ** (-0.5)
    scores = (
        jnp.einsum("qhd,khd->hqk", query_heads, key_block, preferred_element_type=jnp.float32)
        * scale_factor
    )
    position = offset + jnp.arange(key_block.shape[0], dtype=jnp.int32)
    usable = (position < key_limit)[None, None, :]
    masked = jnp.where(usable, scores, lowest_score)
    new_max = jnp.maximum(running_max, jnp.max(masked, axis=2))
    weights = jnp.where(usable, jnp.exp(masked - new_max[:, :, None]), 0.0)
    factor = jnp.exp(running_max - new_max)
    running_mass = running_mass * factor + jnp.sum(weights, axis=2)
    running_sum = running_sum * factor[:, :, None] + jnp.einsum(
        "hqk,khd->hqd",
        weights.astype(jnp.bfloat16),
        value_block,
        preferred_element_type=jnp.float32,
    )
    return (running_sum, new_max, running_mass)


def absorb_blocks(carried, query_heads, key_rows, value_rows, key_limit):
    row_total = key_rows.shape[0]
    block_size = 512
    block_count = row_total // block_size
    key_blocks = key_rows.reshape((block_count, block_size) + key_rows.shape[1:])
    value_blocks = value_rows.reshape((block_count, block_size) + value_rows.shape[1:])

    def absorb_block(running, triple):
        block_number, key_block, value_block = triple
        return (
            absorb(
                running, query_heads, key_block, value_block, block_number * block_size, key_limit
            ),
            None,
        )

    numbers = jnp.arange(block_count, dtype=jnp.int32)
    carried, _ = lax.scan(absorb_block, carried, (numbers, key_blocks, value_blocks))
    return carried


def visit(carried, query_heads, key_rows, value_rows, key_limit):
    return absorb_blocks(carried, query_heads, key_rows, value_rows, key_limit)


def local(queries, keys, values, out_weight, q_gain, k_gain, gate, valid_count):
    row_count = queries.shape[0]
    local_heads = queries.shape[1] // HEAD_DIM
    feature_count = queries.shape[1] * lax.axis_size(("head", "enc"))
    key_limit = valid_count[0]
    query_squares = jnp.sum(jnp.square(queries.astype(jnp.float32)), axis=1)
    key_squares = jnp.sum(jnp.square(keys.astype(jnp.float32)), axis=1)
    query_totals, key_totals = lax.psum((query_squares, key_squares), ("head", "enc"))
    query_heads = normalize(queries, query_totals, q_gain, feature_count).reshape(
        row_count, local_heads, HEAD_DIM
    )
    key_heads = normalize(keys, key_totals, k_gain, feature_count).reshape(
        row_count, local_heads, HEAD_DIM
    )
    value_heads = values.reshape(row_count, local_heads, HEAD_DIM)
    initial = (
        jnp.zeros((local_heads, row_count, HEAD_DIM), jnp.float32),
        jnp.full((local_heads, row_count), lowest_score, jnp.float32),
        jnp.zeros((local_heads, row_count), jnp.float32),
    )
    running_sum, running_max, running_mass = visit(
        initial,
        query_heads,
        lax.all_gather(key_heads, "seq", axis=0, tiled=True),
        lax.all_gather(value_heads, "seq", axis=0, tiled=True),
        key_limit,
    )
    attended = (running_sum / running_mass[:, :, None]).transpose(1, 0, 2)
    attended = attended.reshape(row_count, local_heads * HEAD_DIM).astype(jnp.bfloat16)
    terms = jnp.dot(
        attended,
        lax.all_gather(out_weight, "seq", axis=1, tiled=True),
        preferred_element_type=jnp.float32,
    )
    summed = lax.psum_scatter(
        terms.astype(jnp.bfloat16), ("head", "enc"), scatter_dimension=1, tiled=True
    ).astype(jnp.float32)
    return (gate[None, :] * summed).astype(jnp.bfloat16)


def solution(mesh):
    placed = (
        P("seq", ("head", "enc")),
        P("seq", ("head", "enc")),
        P("seq", ("head", "enc")),
        P(("head", "enc"), "seq"),
        P(("head", "enc")),
        P(("head", "enc")),
        P(("head", "enc")),
        P(),
    )
    return jax.shard_map(
        local, mesh=mesh, in_specs=placed, out_specs=P("seq", ("head", "enc")), check_vma=False
    )
```

profile of v0, /device:TPU:2, one launch (start us, length us, event | category | flops | bytes accessed | tf_op | source)
XLA Modules:
  0.0 957.6 jit_solution(13073559487828346287)
XLA Ops:
  6.5 1.1 fusion.11
  7.6 1.1 fusion.14
  8.7 78.0 %all-reduce = (f32[320]{0:T(512)S(1)}, f32[320]{0:T(512)S(1)}) all-reduce(f32[320]{0:T(512)S(1)} %fusion.11, f32[320]{0:T(512)S(1)} %fusion.14), channel_id=1, replica_groups=mesh['seq'=32,'head'=8,'enc'=2] {'head','enc'}, use_global_device_ids=true, to_apply=%region_1.0 | all-reduce | flops 640 | bytes 5120 | tf_op jit(solution)/shard_map/psum | solution.py:73
  86.7 1.0 fusion.13
  87.7 0.7 reshape.32
  88.5 1.6 reshape.35
  90.2 0.7 all-gather.8.cloned.1.call-update
  91.1 214.0 %all-gather.4.cloned.1.call-done = bf16[10240,2,128]{2,1,0:T(2,128)(2,1)} async-done(((bf16[320,2,128]{2,1,0:T(2,128)(2,1)}), bf16[10240,2,128]{2,1,0:T(2,128)(2,1)}) %all-gather.4.cloned.1.call-update) | async-done | bytes 5242896 | tf_op jit(solution)/shard_map/all_gather | solution.py:89
  305.2 242.4 %all-gather.6.cloned.1.call-done = bf16[10240,2,128]{2,1,0:T(2,128)(2,1)} async-done(((bf16[320,2,128]{2,1,0:T(2,128)(2,1)}), bf16[10240,2,128]{2,1,0:T(2,128)(2,1)}) %all-gather.6.cloned.1.call-update) | async-done | bytes 5242896 | tf_op jit(solution)/shard_map/all_gather | solution.py:90
  547.6 92.4 %while.15 = (s32[]{:T(128)}, f32[2,320,128]{2,1,0:T(8,128)S(1)}, f32[2,320]{1,0:T(2,128)S(1)}, f32[2,320]{1,0:T(2,128)S(1)}, s32[20]{0:T(128)S(1)}, /*index=5*/s...) while((s32[]{:T(128)}, f32[2,320,128]{2,1,0:T(8,128)S(1)}, ...), condition=%wide.region_7.8_spmd.clone, body=%wide.region_4.7_spmd.clone.sunk | while | flops 170971264 | bytes 6367397 | solution.py:58
  548.8 0.7 add_compare_fusion.2
  549.4 1.4 constant_dynamic-slice_fusion.3
  552.2 0.6 dynamic_slice.19
  553.4 0.7 add_compare_fusion.2
  554.1 1.4 constant_dynamic-slice_fusion.3
  556.8 0.6 dynamic_slice.19
  558.0 0.7 add_compare_fusion.2
  558.7 1.4 constant_dynamic-slice_fusion.3
  561.4 0.6 dynamic_slice.19
  562.7 0.7 add_compare_fusion.2
  563.3 1.4 constant_dynamic-slice_fusion.3
  566.0 0.6 dynamic_slice.19
  567.3 0.7 add_compare_fusion.2
  567.9 1.4 constant_dynamic-slice_fusion.3
  570.7 0.6 dynamic_slice.19
  571.9 0.7 add_compare_fusion.2
  572.6 1.4 constant_dynamic-slice_fusion.3
  575.3 0.6 dynamic_slice.19
  576.5 0.7 add_compare_fusion.2
  577.2 1.4 constant_dynamic-slice_fusion.3
  581.2 0.7 add_compare_fusion.2
  581.8 1.4 constant_dynamic-slice_fusion.3
  585.8 0.7 add_compare_fusion.2
  586.4 1.4 constant_dynamic-slice_fusion.3
  589.2 0.6 dynamic_slice.19
  590.4 0.7 add_compare_fusion.2
  591.1 1.4 constant_dynamic-slice_fusion.3
  593.8 0.6 dynamic_slice.19
  595.0 0.7 add_compare_fusion.2
  595.7 1.4 constant_dynamic-slice_fusion.3
  599.6 0.7 add_compare_fusion.2
  600.3 1.4 constant_dynamic-slice_fusion.3
  604.3 0.7 add_compare_fusion.2
  604.9 1.4 constant_dynamic-slice_fusion.3
  608.9 0.7 add_compare_fusion.2
  609.5 1.4 constant_dynamic-slice_fusion.3
  613.5 0.7 add_compare_fusion.2
  614.2 1.4 constant_dynamic-slice_fusion.3
  618.1 0.7 add_compare_fusion.2
  618.8 1.4 constant_dynamic-slice_fusion.3
  622.8 0.7 add_compare_fusion.2
  623.4 1.4 constant_dynamic-slice_fusion.3
  627.4 0.7 add_compare_fusion.2
  628.0 1.4 constant_dynamic-slice_fusion.3
  632.0 0.7 add_compare_fusion.2
  632.7 1.4 constant_dynamic-slice_fusion.3
  636.6 0.7 add_compare_fusion.2
  637.3 1.4 constant_dynamic-slice_fusion.3
  640.0 136.6 %all-gather.8.cloned.1.call-done = bf16[256,5120]{0,1:T(8,128)(2,1)} async-done(((bf16[256,160]{0,1:T(8,128)(2,1)}), bf16[256,5120]{0,1:T(8,128)(2,1)}) %all-gather.8.cloned.1.call-update) | async-done | bytes 2621456 | tf_op jit(solution)/shard_map/all_gather | solution.py:97
  776.6 2.9 convolution_convert_fusion
  779.6 3.6 copy.29
  783.2 166.0 %reduce-scatter.4.cloned.1.call-done = bf16[320,320]{1,0:T(8,128)(2,1)} async-done(((bf16[5120,320]{1,0:T(8,128)(2,1)}), bf16[320,320]{1,0:T(8,128)(2,1)}) %reduce-scatter.4.cloned.1.call-update) | async-done | bytes 204816
  949.2 1.1 copy.30
  950.4 0.7 multiply_convert_fusion
  (153 shorter events, 33.0 us)
Async XLA Ops:
  6.5 84.5 %copy-start.1 = (bf16[320,256]{1,0:T(8,128)(2,1)S(1)}, bf16[320,256]{1,0:T(8,128)(2,1)}, u32[]{:S(2)}) copy-start(bf16[320,256]{1,0:T(8,128)(2,1)} %param.10) | copy-start | bytes 491524
  6.5 84.5 %copy-start.3 = (f32[256]{0:T(256)S(1)}, f32[256]{0:T(256)}, u32[]{:S(2)}) copy-start(f32[256]{0:T(256)} %param.14) | copy-start | bytes 3076
  6.5 298.6 %all-gather.4.cloned.1.call-start = ((), (), s32[]{:S(2)}) async-start(), calls=%async_computation.1 | async-start | bytes 5406720 | tf_op jit(solution)/shard_map/all_gather | solution.py:89
  88.5 459.1 %all-gather.6.cloned.1.call-start = ((), (), s32[]{:S(2)}) async-start(), calls=%async_computation.2 | async-start | bytes 5406720 | tf_op jit(solution)/shard_map/all_gather | solution.py:90
  90.2 686.4 %all-gather.8.cloned.1.call-start = ((), (), s32[]{:S(2)}) async-start(), calls=%async_computation.3 | async-start | bytes 2703360 | tf_op jit(solution)/shard_map/all_gather | solution.py:97
  90.9 858.3 %reduce-scatter.4.cloned.1.call-start = ((), (), s32[]{:S(2)}) async-start(), calls=%async_computation.4 | async-start | bytes 4177920
  640.0 136.6 %copy-start = (f32[2,320,128]{2,1,0:T(8,128)}, f32[2,320,128]{2,1,0:T(8,128)S(1)}, u32[]{:S(2)}) copy-start(f32[2,320,128]{2,1,0:T(8,128)S(1)} %get-tuple-element.53) | copy-start | bytes 983044
  783.2 167.2 %copy-start.2 = (f32[320]{0:T(512)S(1)}, f32[320]{0:T(512)}, u32[]{:S(2)}) copy-start(f32[320]{0:T(512)} %param.16) | copy-start | bytes 3844
Sparse Core Ops, SparseCore 0:
  88.6 216.5 all-gather.3
  307.2 240.2 all-gather.5
  549.6 226.9 all-gather.7
  783.4 165.8 reduce-scatter.3
where the time goes:
time: 959 us; the launch traced here: 958 us
  waiting for transfers between devices  760 us (79%)
  blocking collectives  78 us (8%)
  local copies, waits for them, and re-layouts  46.8 us (5%)
  other arithmetic  25.5 us (3%)
  matrix products  20.2 us (2%)
  loops' own time  14.1 us (1%)
  between operations  13.2 us (1%)
    all_gather x1, waiting for transfers between devices, local(): lax.all_gather(value_heads, 'seq', axis=0, tiled=True)  242 us
    all_gather x1, waiting for transfers between devices, local(): lax.all_gather(key_heads, 'seq', axis=0, tiled=True)  214 us
    unnamed x5, waiting for transfers between devices  167 us
    all_gather x1, waiting for transfers between devices, local(): lax.all_gather(out_weight, 'seq', axis=1, tiled=True)  137 us
    psum x1, blocking collectives, local(): lax.psum((query_squares, key_squares), ('head', 'enc'))  78 us
    dynamic_slice x40, local copies, waits for them, and re-layouts, absorb_blocks(): lax.scan(absorb_block, carried, (numbers, key_blocks, value_blocks))  39.7 us
  transfers between devices with their start and end apart: 4, of which 4 were waited for; matrix products, arithmetic and copies ran while one was open for 8% of the time, Pallas kernels for 0%

commit v1 on v0

--- a/solution.py
+++ b/solution.py
@@ -70,7 +70,7 @@
     key_limit = valid_count[0]
     query_squares = jnp.sum(jnp.square(queries.astype(jnp.float32)), axis=1)
     key_squares = jnp.sum(jnp.square(keys.astype(jnp.float32)), axis=1)
-    query_totals, key_totals = lax.psum((query_squares, key_squares), ("head", "enc"))
+    query_totals, key_totals = lax.psum(lax.psum((query_squares, key_squares), "enc"), "head")
     query_heads = normalize(queries, query_totals, q_gain, feature_count).reshape(
         row_count, local_heads, HEAD_DIM
     )

time: 959 us -> 917 us (0.956)
  blocking collectives: 78 us -> 30.7 us
    psum x1 -> x2, blocking collectives: 78 us -> 30.7 us  [the longest x1 16.7 us: local(): lax.psum((query_squares, key_squares), 'enc')]
  transfers between devices with their start and end apart: 4 -> 4, of which waited for: 4 -> 4; matrix products, arithmetic and copies ran while one was open for 8% -> 9% of each run, Pallas kernels for 0% -> 0%
where the time goes in v1:
time: 917 us; the launch traced here: 916 us
  waiting for transfers between devices  767 us (84%)
  local copies, waits for them, and re-layouts  46.8 us (5%)
  blocking collectives  30.7 us (3%)
  other arithmetic  24.5 us (3%)
  matrix products  20.2 us (2%)
  loops' own time  14.1 us (2%)
  between operations  13.2 us (1%)
    all_gather x1, waiting for transfers between devices, local(): lax.all_gather(value_heads, 'seq', axis=0, tiled=True)  242 us
    all_gather x1, waiting for transfers between devices, local(): lax.all_gather(key_heads, 'seq', axis=0, tiled=True)  221 us
    unnamed x5, waiting for transfers between devices  167 us
    all_gather x1, waiting for transfers between devices, local(): lax.all_gather(out_weight, 'seq', axis=1, tiled=True)  137 us
    dynamic_slice x40, local copies, waits for them, and re-layouts, absorb_blocks(): lax.scan(absorb_block, carried, (numbers, key_blocks, value_blocks))  39.7 us
  transfers between devices with their start and end apart: 4, of which 4 were waited for; matrix products, arithmetic and copies ran while one was open for 9% of the time, Pallas kernels for 0%

profile of v1, /device:TPU:2, one launch (start us, length us, event | category | flops | bytes accessed | tf_op | source)
XLA Modules:
  0.0 916.4 jit_solution(7844708087662312824)
XLA Ops:
  6.5 1.2 fusion.11
  7.8 16.7 %all-reduce.1 = (f32[320]{0:T(512)S(1)}, f32[320]{0:T(512)S(1)}) all-reduce(f32[320]{0:T(512)S(1)} %get-tuple-element.140, f32[320]{0:T(512)S(1)} %get-tuple-element.141), channel_id=1, replica_groups=mesh['seq'=32,'head'=8,'enc'=2] {'enc'}, use_global_device_ids=true, to_apply=%region_1.0 | all-reduce | flops 640 | bytes 5120 | tf_op jit(solution)/shard_map/psum | solution.py:73
  24.5 14.0 %all-reduce = (f32[320]{0:T(512)S(1)}, f32[320]{0:T(512)S(1)}) all-reduce(f32[320]{0:T(512)S(1)} %get-tuple-element.132, f32[320]{0:T(512)S(1)} %get-tuple-element.133), channel_id=1, replica_groups=mesh['seq'=32,'head'=8,'enc'=2] {'head'}, use_global_device_ids=true, to_apply=%region_2.0 | all-reduce | flops 640 | bytes 5120 | tf_op jit(solution)/shard_map/psum | solution.py:73
  38.5 1.0 fusion.13
  39.5 0.7 reshape.32
  40.3 1.6 reshape.35
  42.0 0.7 all-gather.8.cloned.1.call-update
  42.9 220.9 %all-gather.4.cloned.1.call-done = bf16[10240,2,128]{2,1,0:T(2,128)(2,1)} async-done(((bf16[320,2,128]{2,1,0:T(2,128)(2,1)}), bf16[10240,2,128]{2,1,0:T(2,128)(2,1)}) %all-gather.4.cloned.1.call-update) | async-done | bytes 5242896 | tf_op jit(solution)/shard_map/all_gather | solution.py:89
  263.8 242.4 %all-gather.6.cloned.1.call-done = bf16[10240,2,128]{2,1,0:T(2,128)(2,1)} async-done(((bf16[320,2,128]{2,1,0:T(2,128)(2,1)}), bf16[10240,2,128]{2,1,0:T(2,128)(2,1)}) %all-gather.6.cloned.1.call-update) | async-done | bytes 5242896 | tf_op jit(solution)/shard_map/all_gather | solution.py:90
  506.2 92.4 %while.15 = (s32[]{:T(128)}, f32[2,320,128]{2,1,0:T(8,128)S(1)}, f32[2,320]{1,0:T(2,128)S(1)}, f32[2,320]{1,0:T(2,128)S(1)}, s32[20]{0:T(128)S(1)}, /*index=5*/s...) while((s32[]{:T(128)}, f32[2,320,128]{2,1,0:T(8,128)S(1)}, ...), condition=%wide.region_9.10_spmd.clone, body=%wide.region_6.9_spmd.clone.sunk | while | flops 170971264 | bytes 6367397 | solution.py:58
  507.4 0.7 add_compare_fusion.2
  508.1 1.4 constant_dynamic-slice_fusion.3
  512.0 0.7 add_compare_fusion.2
  512.7 1.4 constant_dynamic-slice_fusion.3
  516.7 0.7 add_compare_fusion.2
  517.3 1.4 constant_dynamic-slice_fusion.3
  520.0 0.6 dynamic_slice.19
  521.3 0.7 add_compare_fusion.2
  521.9 1.4 constant_dynamic-slice_fusion.3
  524.7 0.6 dynamic_slice.19
  525.9 0.7 add_compare_fusion.2
  526.6 1.4 constant_dynamic-slice_fusion.3
  529.3 0.6 dynamic_slice.19
  530.5 0.7 add_compare_fusion.2
  531.2 1.4 constant_dynamic-slice_fusion.3
  533.9 0.6 dynamic_slice.19
  535.1 0.7 add_compare_fusion.2
  535.8 1.4 constant_dynamic-slice_fusion.3
  538.5 0.6 dynamic_slice.19
  539.8 0.7 add_compare_fusion.2
  540.4 1.4 constant_dynamic-slice_fusion.3
  543.2 0.6 dynamic_slice.19
  544.4 0.7 add_compare_fusion.2
  545.1 1.4 constant_dynamic-slice_fusion.3
  547.8 0.6 dynamic_slice.19
  549.0 0.7 add_compare_fusion.2
  549.7 1.4 constant_dynamic-slice_fusion.3
  552.4 0.6 dynamic_slice.19
  553.6 0.7 add_compare_fusion.2
  554.3 1.4 constant_dynamic-slice_fusion.3
  558.3 0.7 add_compare_fusion.2
  558.9 1.4 constant_dynamic-slice_fusion.3
  562.9 0.7 add_compare_fusion.2
  563.5 1.4 constant_dynamic-slice_fusion.3
  567.5 0.7 add_compare_fusion.2
  568.2 1.4 constant_dynamic-slice_fusion.3
  572.1 0.7 add_compare_fusion.2
  572.8 1.4 constant_dynamic-slice_fusion.3
  576.8 0.7 add_compare_fusion.2
  577.4 1.4 constant_dynamic-slice_fusion.3
  581.4 0.7 add_compare_fusion.2
  582.0 1.4 constant_dynamic-slice_fusion.3
  586.0 0.7 add_compare_fusion.2
  586.7 1.4 constant_dynamic-slice_fusion.3
  590.6 0.7 add_compare_fusion.2
  591.3 1.4 constant_dynamic-slice_fusion.3
  595.2 0.7 add_compare_fusion.2
  595.9 1.4 constant_dynamic-slice_fusion.3
  598.6 136.7 %all-gather.8.cloned.1.call-done = bf16[256,5120]{0,1:T(8,128)(2,1)} async-done(((bf16[256,160]{0,1:T(8,128)(2,1)}), bf16[256,5120]{0,1:T(8,128)(2,1)}) %all-gather.8.cloned.1.call-update) | async-done | bytes 2621456 | tf_op jit(solution)/shard_map/all_gather | solution.py:97
  735.3 2.9 convolution_convert_fusion
  738.2 3.6 copy.29
  741.9 166.1 %reduce-scatter.4.cloned.1.call-done = bf16[320,320]{1,0:T(8,128)(2,1)} async-done(((bf16[5120,320]{1,0:T(8,128)(2,1)}), bf16[320,320]{1,0:T(8,128)(2,1)}) %reduce-scatter.4.cloned.1.call-update) | async-done | bytes 204816
  907.9 1.1 copy.30
  909.1 0.7 multiply_convert_fusion
  (154 shorter events, 33.0 us)
Async XLA Ops:
  6.5 36.2 %copy-start.1 = (bf16[320,256]{1,0:T(8,128)(2,1)S(1)}, bf16[320,256]{1,0:T(8,128)(2,1)}, u32[]{:S(2)}) copy-start(bf16[320,256]{1,0:T(8,128)(2,1)} %param.10) | copy-start | bytes 491524
  6.5 36.2 %copy-start.3 = (f32[256]{0:T(256)S(1)}, f32[256]{0:T(256)}, u32[]{:S(2)}) copy-start(f32[256]{0:T(256)} %param.14) | copy-start | bytes 3076
  6.5 257.2 %all-gather.4.cloned.1.call-start = ((), (), s32[]{:S(2)}) async-start(), calls=%async_computation.1 | async-start | bytes 5406720 | tf_op jit(solution)/shard_map/all_gather | solution.py:89
  40.2 465.9 %all-gather.6.cloned.1.call-start = ((), (), s32[]{:S(2)}) async-start(), calls=%async_computation.2 | async-start | bytes 5406720 | tf_op jit(solution)/shard_map/all_gather | solution.py:90
  41.9 693.4 %all-gather.8.cloned.1.call-start = ((), (), s32[]{:S(2)}) async-start(), calls=%async_computation.3 | async-start | bytes 2703360 | tf_op jit(solution)/shard_map/all_gather | solution.py:97
  42.7 865.3 %reduce-scatter.4.cloned.1.call-start = ((), (), s32[]{:S(2)}) async-start(), calls=%async_computation.4 | async-start | bytes 4177920
  598.6 136.7 %copy-start = (f32[2,320,128]{2,1,0:T(8,128)}, f32[2,320,128]{2,1,0:T(8,128)S(1)}, u32[]{:S(2)}) copy-start(f32[2,320,128]{2,1,0:T(8,128)S(1)} %get-tuple-element.53) | copy-start | bytes 983044
  741.9 167.2 %copy-start.2 = (f32[320]{0:T(512)S(1)}, f32[320]{0:T(512)}, u32[]{:S(2)}) copy-start(f32[320]{0:T(512)} %param.16) | copy-start | bytes 3844
Sparse Core Ops, SparseCore 0:
  40.4 223.3 all-gather.3
  265.8 240.2 all-gather.5
  508.3 226.9 all-gather.7
  742.0 165.8 reduce-scatter.3
